TPU v7x, 256 devices: a whole 4x4x8 slice. The times are simulated.
256 devices in a mesh: ctx: 32 (over y, z_lo, x), exp: 8 (over z_hi, core).
Axes of the slice: x: 4, y: 4, z: 8 (z_hi: 4, z_lo: 2; z = z_hi * 2 + z_lo), core: 2. Of those that a mesh axis runs over, the one named last changes fastest.
Arguments:
- lin_query: bfloat16 [4096, 8192], P('ctx', 'exp'), may hold values from -5 to 5
- lin_key: bfloat16 [4096, 8192], P('ctx', 'exp'), may hold values from -5 to 5
- lin_value: bfloat16 [4096, 8192], P('ctx', 'exp'), may hold values from -5 to 5
- log_decay: float32 [4096, 64], P('ctx', 'exp'), may hold values from -1.5 to 0
- lin_gain: float32 [8192], P('exp'), may hold values from 0.25 to 1.75
- moe_input: bfloat16 [1536, 6144], P(('ctx', 'exp')), may hold values from -6 to 6
- routes: int32 [1536, 2], P(('ctx', 'exp')), may hold values from 0 to 7, all different within a row; in each aligned block of 6 rows (0 to 5, 6 to 11, ...) at most 2 rows name the same one
- route_weight: float32 [1536, 2], P(('ctx', 'exp')), may hold values from 0.2 to 1
- gate_weight: bfloat16 [8, 6144, 9216], P('exp', None, 'ctx'), may hold values from -0.078125 to 0.078125
- up_weight: bfloat16 [8, 6144, 9216], P('exp', None, 'ctx'), may hold values from -0.078125 to 0.078125
- down_weight: bfloat16 [8, 9216, 6144], P('exp', 'ctx'), may hold values from -0.0625 to 0.0625
- soft_query: bfloat16 [4096, 8192], P('ctx', 'exp'), may hold values from -5 to 5
- soft_kv: bfloat16 [4096, 8, 2, 128], P('ctx', 'exp'), may hold values from -5 to 5
Outputs:
- lin_out: bfloat16 [4096, 8192], P('ctx', 'exp')
- moe_out: bfloat16 [1536, 6144], P(('ctx', 'exp'))
- soft_out: bfloat16 [4096, 8192], P('ctx', 'exp')
Inputs may be any that keep to these rules, and one draw needn't show every extreme that they name: `routes`: within the rows of one device (6 rows) each expert is named by at most 2 of them; the 2 experts of a row differ.
All inputs are finite; a program needn't handle non-finite values.
Results may differ from a plain program's by a relative error of at most 0.009.
Values may be sent and summed in bfloat16 or wider, within the bound.
A program may use at most 128 MiB of HBM per device.

v0:
```python
import math
import jax
import jax.numpy as jnp
from jax import lax
from jax.sharding import PartitionSpec as P

D = 6144
HEAD_TOTAL = 64
HEAD = 128
KV_HEADS = 8
EXPERTS = 8
TOP = 2
CAP = 2


def prefix(value, axis, join, neutral):
    count, mine = (lax.axis_size(axis), lax.axis_index(axis))
    pieces = jax.tree.map(lambda part: lax.all_gather(part, axis), value)
    so_far = jax.tree.map(
        lambda part, zero: jnp.full_like(part, 0) + jnp.asarray(zero, part.dtype), value, neutral
    )

    def hop(position, so_far):
        longer = join(so_far, jax.tree.map(lambda part: part[position], pieces))
        return jax.tree.map(lambda new, old: jnp.where(position < mine, new, old), longer, so_far)

    return lax.fori_loop(0, count - 1, hop, so_far)


def lightning(lin_query, lin_key, lin_value, log_decay, lin_gain):
    length = lin_query.shape[0]
    heads_here = log_decay.shape[1]
    score_scale = 1.0 / math.sqrt(HEAD)
    queries = lin_query.reshape(length, heads_here, HEAD)
    key_rows = lin_key.reshape(length, heads_here, HEAD)
    value_f = lin_value.reshape(length, heads_here, HEAD).astype(jnp.float32)
    cumulative = jnp.cumsum(log_decay, axis=0)
    scores = (
        jnp.einsum("thd,jhd->htj", queries, key_rows, preferred_element_type=jnp.float32)
        * score_scale
    )
    spread = cumulative.T[:, :, None] - cumulative.T[:, None, :]
    causal = jnp.tril(jnp.ones((length, length), dtype=jnp.bool_))
    decays = jnp.where(causal[None], jnp.exp(jnp.where(causal[None], spread, 0.0)), 0.0)
    within = jnp.einsum("htj,jhd->thd", scores * decays, value_f, precision=lax.Precision.HIGHEST)
    tail_decay = jnp.exp(cumulative[-1][None, :] - cumulative)
    local_state = jnp.einsum(
        "th,thd,the->hde",
        tail_decay,
        key_rows.astype(jnp.float32),
        value_f,
        precision=lax.Precision.HIGHEST,
    )

    def combine(earlier, latter):
        return (earlier[0] + latter[0], jnp.exp(latter[0])[:, None, None] * earlier[1] + latter[1])

    identity = (
        jnp.zeros((heads_here,), jnp.float32),
        jnp.zeros((heads_here, HEAD, HEAD), jnp.float32),
    )
    prior_log, prior_state = prefix((cumulative[-1], local_state), "ctx", combine, identity)
    carried = (
        jnp.exp(cumulative)[:, :, None]
        * jnp.einsum(
            "thd,hde->the",
            queries.astype(jnp.float32),
            prior_state,
            precision=lax.Precision.HIGHEST,
        )
        * score_scale
    )
    combined = within + carried
    root_mean = jnp.sqrt(jnp.mean(combined * combined, axis=-1, keepdims=True) + 1e-06)
    normed = combined / root_mean * lin_gain.reshape(heads_here, HEAD)
    return normed.reshape(length, heads_here * HEAD).astype(jnp.bfloat16)


def experts_layer(moe_input, routes, route_weight, gate_weight, up_weight, down_weight):
    row_count = moe_input.shape[0]
    pair_count = row_count * TOP
    flat_ids = routes.reshape(pair_count)
    same_expert = flat_ids[:, None] == flat_ids[None, :]
    pair_order = jnp.arange(pair_count, dtype=jnp.int32)
    earlier_pair = pair_order[None, :] < pair_order[:, None]
    slot_rank = jnp.sum(jnp.logical_and(same_expert, earlier_pair), axis=1)
    slot_index = slot_rank * EXPERTS + flat_ids
    onehot = (slot_index[None, :] == jnp.arange(CAP * EXPERTS, dtype=jnp.int32)[:, None]).astype(
        jnp.bfloat16
    )
    pair_rows = jnp.repeat(moe_input, TOP, axis=0)
    outgoing = (
        jnp.dot(onehot, pair_rows, preferred_element_type=jnp.float32)
        .astype(jnp.bfloat16)
        .reshape(CAP, EXPERTS, D)
    )
    arrived = lax.all_to_all(outgoing, "exp", split_axis=1, concat_axis=0, tiled=True)
    shard_piece = lax.all_gather(arrived, "ctx", axis=0, tiled=True)
    gate_part = jnp.einsum(
        "red,edf->ref", shard_piece, gate_weight, preferred_element_type=jnp.float32
    )
    up_part = jnp.einsum("red,edf->ref", shard_piece, up_weight, preferred_element_type=jnp.float32)
    hidden = (jax.nn.silu(gate_part) * up_part).astype(jnp.bfloat16)
    expert_out = lax.psum_scatter(
        jnp.einsum("ref,efd->red", hidden, down_weight, preferred_element_type=jnp.float32),
        "ctx",
        scatter_dimension=0,
        tiled=True,
    ).astype(jnp.bfloat16)
    returned = lax.all_to_all(expert_out, "exp", split_axis=0, concat_axis=1, tiled=True).reshape(
        CAP * EXPERTS, D
    )
    pair_out = jnp.dot(onehot.T, returned, preferred_element_type=jnp.float32).reshape(
        row_count, TOP, D
    )
    mixed = jnp.sum(pair_out * route_weight[:, :, None], axis=1)
    return mixed.astype(jnp.bfloat16)


def softmax_layer(soft_query, soft_kv):
    length = soft_query.shape[0]
    kv_here = soft_kv.shape[1]
    group = HEAD_TOTAL // KV_HEADS
    score_scale = 1.0 / math.sqrt(HEAD)
    queries = soft_query.reshape(length, kv_here, group, HEAD)
    query_pos = lax.axis_index("ctx") * length + jnp.arange(length, dtype=jnp.int32)
    shard_piece = lax.all_gather(soft_kv, "ctx", axis=0, tiled=True)
    maxima = jnp.full((kv_here, group, length), -jnp.inf, jnp.float32)
    totals = jnp.zeros((kv_here, group, length), jnp.float32)
    running = jnp.zeros((kv_here, group, length, HEAD), jnp.float32)
    key_rows = shard_piece[:, :, 0, :]
    value_rows = shard_piece[:, :, 1, :]
    key_pos = jnp.arange(shard_piece.shape[0], dtype=jnp.int32)
    scores = (
        jnp.einsum("tghd,jgd->ghtj", queries, key_rows, preferred_element_type=jnp.float32)
        * score_scale
    )
    allowed = key_pos[None, :] <= query_pos[:, None]
    scores = jnp.where(allowed[None, None], scores, -jnp.inf)
    new_max = jnp.max(scores, axis=-1)
    safe_max = jnp.where(jnp.isfinite(new_max), new_max, 0.0)
    shrink = jnp.exp(maxima - safe_max)
    weights = jnp.exp(scores - safe_max[..., None])
    totals = totals * shrink + jnp.sum(weights, axis=-1)
    update = jnp.einsum(
        "ghtj,jgd->ghtd",
        weights.astype(jnp.bfloat16),
        value_rows,
        preferred_element_type=jnp.float32,
    )
    running = running * shrink[..., None] + update
    output = running / totals[..., None]
    return output.transpose(2, 0, 1, 3).reshape(length, kv_here * group * HEAD).astype(jnp.bfloat16)


def on_device(
    lin_query,
    lin_key,
    lin_value,
    log_decay,
    lin_gain,
    moe_input,
    routes,
    route_weight,
    gate_weight,
    up_weight,
    down_weight,
    soft_query,
    soft_kv,
):
    lin_out = lightning(lin_query, lin_key, lin_value, log_decay, lin_gain)
    soft_out = softmax_layer(soft_query, soft_kv)
    moe_out = experts_layer(moe_input, routes, route_weight, gate_weight, up_weight, down_weight)
    return (lin_out, moe_out, soft_out)


def solution(mesh):
    placed = (
        P("ctx", "exp"),
        P("ctx", "exp"),
        P("ctx", "exp"),
        P("ctx", "exp"),
        P("exp"),
        P(("ctx", "exp"), None),
        P(("ctx", "exp"), None),
        P(("ctx", "exp"), None),
        P("exp", None, "ctx"),
        P("exp", None, "ctx"),
        P("exp", "ctx", None),
        P("ctx", "exp"),
        P("ctx", "exp", None, None),
    )
    return jax.shard_map(
        on_device,
        mesh=mesh,
        in_specs=placed,
        out_specs=(P("ctx", "exp"), P(("ctx", "exp"), None), P("ctx", "exp")),
        check_vma=False,
    )
```

profile of v0, /device:TPU:1, one launch (start us, length us, event | category | flops | bytes accessed | tf_op | source)
XLA Modules:
  0.0 780.1 jit_solution(14892325670164838628)
XLA Ops:
  13.0 18.5 %all_to_all.33 = bf16[2,8,6144]{2,0,1:T(2,128)(2,1)} all-to-all(bf16[2,8,6144]{2,0,1:T(2,128)(2,1)S(1)} %copy.120), channel_id=1, replica_groups=mesh['ctx'=32,'exp'=8] {'exp'}, dimensions={1} | all-to-all | bytes 393216 | tf_op jit(solution)/shard_map/all_to_all | solution.py:97
  43.3 2.2 fusion.56
  45.6 132.8 %all-gather.6.cloned.1.call-done = bf16[512,1,6144]{2,0,1:T(8,128)(2,1)} async-done(((bf16[16,1,6144]{2,0,1:T(8,128)(2,1)}), bf16[512,1,6144]{2,0,1:T(8,128)(2,1)}) %all-gather.6.cloned.1.call-update) | async-done | bytes 6291472 | tf_op jit(solution)/shard_map/all_gather | solution.py:98
  178.4 6.0 fusion.16
  187.1 6.4 convolution_bitcast_fusion
  194.6 68.3 %all-gather.1 = f32[32,1,8]{2,1,0:T(1,128)} all-gather(f32[1,1,8]{2,1,0:T(1,128)S(1)} %copy-done.7), channel_id=1, replica_groups=mesh['ctx'=32,'exp'=8] {'ctx'}, dimensions={0}, use_global_device_ids=true | all-gather | bytes 1056 | tf_op jit(solution)/shard_map/all_gather | solution.py:18
  264.4 69.8 %all-gather.8.cloned.1.call-done = bf16[4096,1,2,128]{3,0,2,1:T(8,128)(2,1)} async-done(((bf16[128,1,2,128]{3,0,2,1:T(8,128)(2,1)}), bf16[4096,1,2,128]{3,0,2,1:T(8,128)(2,1)}) %all-gather.8.cloned.1.call-update) | async-done | bytes 2097168 | tf_op jit(solution)/shard_map/all_gather | solution.py:127
  334.2 8.2 %fusion.3 = (f32[8,128]{1,0:T(8,128)S(1)}, f32[4096,128,8]{1,0,2:T(8,128)}) fusion(pred[128,4096]{0,1:T(8,128)(4,1)S(1)} %iota_compare_fusion, bf16[4096,1,2,128]{3,0,2,1:T(8,128)(2,1)} %all-gather.8.cloned.1.call-done, bf16[128,1024]{1,0:T(8,128)(2,1)S(1)} %copy-done.11), kind=kOutput, calls=%fused_computation.7 | convolution fusion | flops 1086323712 | bytes 18616320 | tf_op jit(solution)/shard_map/tghd,jgd->ghtj/dot_general | solution.py:135
  342.4 9.3 %fusion.1 = f32[8,128]{1,0:T(8,128)S(1)} fusion(f32[4096,128,8]{1,0,2:T(8,128)} %get-tuple-element.152, f32[8,128]{1,0:T(8,128)S(1)} %is-finite_select_fusion, pred[128,4096]{0,1:T(8,128)(4,1)S(1)} %iota_compare_fusion), kind=kLoop, calls=%fused_computation.5 | loop fusion | flops 16776192 | bytes 17309696 | tf_op jit(solution)/shard_map/reduce_sum | solution.py:144
  351.8 8.6 %fusion.53 = bf16[8,128,128]{1,2,0:T(8,128)(2,1)} fusion(bf16[4096,1,2,128]{3,0,2,1:T(8,128)(2,1)S(1)} %copy-done.10, f32[4096,128,8]{1,0,2:T(8,128)} %get-tuple-element.152, f32[8,128]{1,0:T(8,128)S(1)} %is-finite_select_fusion, pred[128,4096]{0,1:T(8,128)(4,1)S(1)} %iota_compare_fusion, f32[8,128]{1,0:T(8,128)S(1)} %get-tuple-element.146, ...), kind=kOutput, calls=%fused_computation.41 | convolution fusion | flops 1090912256 | bytes 18624512 | tf_op jit(solution)/shard_map/ghtj,jgd->ghtd/dot_general | solution.py:145
  362.3 183.9 %all-gather.10.cloned.1.call-done = f32[256,128,128]{2,1,0:T(8,128)} async-done(((f32[8,128,128]{2,1,0:T(8,128)}), f32[256,128,128]{2,1,0:T(8,128)}) %all-gather.10.cloned.1.call-update) | async-done | bytes 16777232 | tf_op jit(solution)/shard_map/all_gather | solution.py:18
  546.2 87.4 %while.14 = (s32[]{:T(128)}, f32[8,128,128]{2,1,0:T(8,128)}, s32[]{:T(128)}, f32[32,8]{1,0:T(8,128)}, f32[32,8,128,128]{3,2,1,0:T(8,128)}, /*index=5*/s32[]{:T(128)}, s32[]{:T(128)}) while((s32[]{:T(128)}, f32[8,128,128]{2,1,0:T(8,128)}, s32[]{:T(128)}, f32[32,8]{1,0:T(8,128)}, f32[32,8,128,128]{3,2,1,0:T(8,128)}, ...), condition=%wide.region_2.3_spmd.clone, body=%wide.region_1.2_spmd.clone.sunk | while | flops 524292 | bytes 1573065 | solution.py:27
  549.5 2.1 fusion.93
  552.4 2.1 fusion.93
  555.2 2.1 fusion.93
  558.0 2.1 fusion.93
  560.8 2.1 fusion.93
  563.6 2.1 fusion.93
  566.5 2.1 fusion.93
  569.3 2.1 fusion.93
  572.1 2.1 fusion.93
  575.0 2.1 fusion.93
  577.8 2.1 fusion.93
  580.6 2.1 fusion.93
  583.4 2.1 fusion.93
  586.3 2.1 fusion.93
  589.1 2.1 fusion.93
  591.9 2.1 fusion.93
  594.8 2.1 fusion.93
  597.6 2.1 fusion.93
  600.4 2.1 fusion.93
  603.2 2.1 fusion.93
  608.9 2.1 fusion.93
  611.7 2.1 fusion.93
  614.5 2.1 fusion.93
  617.3 2.1 fusion.93
  620.1 2.1 fusion.93
  623.0 2.1 fusion.93
  625.8 2.1 fusion.93
  628.6 2.1 fusion.93
  631.4 2.1 fusion.93
  635.3 2.6 multiply_reduce_fusion
  637.9 84.6 %reduce-scatter.2.cloned.1.call-done = f32[16,1,6144]{2,0,1:T(8,128)} async-done(((f32[512,1,6144]{2,0,1:T(8,128)}), f32[16,1,6144]{2,0,1:T(8,128)}) %reduce-scatter.2.cloned.1.call-update) | async-done | bytes 393232 | tf_op jit(solution)/shard_map/reduce_scatter | solution.py:104
  724.7 2.3 reduce.3
  728.8 27.5 %all-to-all-start.1 = ((bf16[8,2,6144]{2,1,0:T(2,128)(2,1)}), bf16[8,2,6144]{2,1,0:T(2,128)(2,1)}, u32[]{:S(2)}, u32[]{:S(2)}) async-start(bf16[8,2,6144]{2,1,0:T(2,128)(2,1)} %reshape.218), calls=%async_computation.2 | async-start | bytes 393216 | tf_op jit(solution)/shard_map/all_to_all | solution.py:110
  760.0 5.0 all-to-all-done.1
  764.9 2.2 reshape.219
  767.2 2.8 reduce.2
  (104 shorter events, 63.1 us)
Async XLA Ops:
  7.2 179.9 %copy-start = (bf16[1,288,6144]{2,1,0:T(8,128)(2,1)S(1)}, bf16[1,288,6144]{2,1,0:T(8,128)(2,1)}, u32[]{:S(2)}) copy-start(bf16[1,288,6144]{2,1,0:T(8,128)(2,1)} %param.25) | copy-start | bytes 10616836
  7.2 171.2 %all-gather.6.cloned.1.call-start = ((), (), s32[]{:S(2)}) async-start(), calls=%async_computation.3 | async-start | bytes 6488064 | tf_op jit(solution)/shard_map/all_gather | solution.py:98
  33.3 301.0 %all-gather.8.cloned.1.call-start = ((), (), s32[]{:S(2)}) async-start(), calls=%async_computation.5 | async-start | bytes 2162688 | tf_op jit(solution)/shard_map/all_gather | solution.py:127
  34.8 511.4 %all-gather.10.cloned.1.call-start = ((), (), s32[]{:S(2)}) async-start(), calls=%async_computation.6 | async-start | bytes 17301504 | tf_op jit(solution)/shard_map/all_gather | solution.py:18
  45.6 676.9 %reduce-scatter.2.cloned.1.call-start = ((), (), s32[]{:S(2)}) async-start(), calls=%async_computation.4 | async-start | bytes 12976128 | tf_op jit(solution)/shard_map/reduce_scatter | solution.py:104
  178.4 6.0 copy-start.8
  178.4 6.6 copy-start.9
  193.5 0.8 copy-start.5
  193.5 0.9 copy-start.3
  193.5 1.1 copy-start.7
  193.5 69.5 %copy-start.2 = (bf16[128,1024]{0,1:T(8,128)(2,1)S(1)}, bf16[128,1024]{0,1:T(8,128)(2,1)}, u32[]{:S(2)}) copy-start(bf16[128,1024]{0,1:T(8,128)(2,1)} %copy.134) | copy-start | bytes 786436
  193.5 69.5 %copy-start.4 = (bf16[128,1024]{1,0:T(8,128)(2,1)S(1)}, bf16[128,1024]{1,0:T(8,128)(2,1)}, u32[]{:S(2)}) copy-start(bf16[128,1024]{1,0:T(8,128)(2,1)} %param.15) | copy-start | bytes 786436
  193.5 140.7 %copy-start.11 = (bf16[128,1024]{1,0:T(8,128)(2,1)S(1)}, bf16[128,1024]{1,0:T(8,128)(2,1)}, u32[]{:S(2)}) copy-start(bf16[128,1024]{1,0:T(8,128)(2,1)} %param.26) | copy-start | bytes 786436
  342.4 9.3 %copy-start.10 = (bf16[4096,1,2,128]{3,0,2,1:T(8,128)(2,1)S(1)}, bf16[4096,1,2,128]{3,0,2,1:T(8,128)(2,1)}, u32[]{:S(2)}) copy-start(bf16[4096,1,2,128]{3,0,2,1:T(8,128)(2,1)} %all-gather.8.cloned.1.call-done) | copy-start | bytes 6291460
  360.3 395.9 %copy-start.6 = (f32[1024]{0:T(1024)S(1)}, f32[1024]{0:T(1024)}, u32[]{:S(2)}) copy-start(f32[1024]{0:T(1024)} %param.19) | copy-start | bytes 12292
  360.3 413.2 %copy-start.1 = (bf16[1,288,6144]{2,1,0:T(8,128)(2,1)S(1)}, bf16[1,288,6144]{2,1,0:T(8,128)(2,1)}, u32[]{:S(2)}) copy-start(bf16[1,288,6144]{2,1,0:T(8,128)(2,1)} %param.25) | copy-start | bytes 10616836
  728.8 36.2 %all-to-all-start.1 = ((bf16[8,2,6144]{2,1,0:T(2,128)(2,1)}), bf16[8,2,6144]{2,1,0:T(2,128)(2,1)}, u32[]{:S(2)}, u32[]{:S(2)}) async-start(bf16[8,2,6144]{2,1,0:T(2,128)(2,1)} %reshape.218), calls=%async_computation.2 | async-start | bytes 393216 | tf_op jit(solution)/shard_map/all_to_all | solution.py:110
Sparse Core Ops, SparseCore 0:
  33.4 144.9 all-gather.5
  180.2 153.9 all-gather.7
  336.0 210.1 all-gather.9
  548.6 173.8 reduce-scatter.1
where the time goes:
time: 783 us; the launch traced here: 780 us
  waiting for transfers between devices  476 us (61%)
  other arithmetic  87.9 us (11%)
  blocking collectives  86.9 us (11%)
  local copies, waits for them, and re-layouts  45.9 us (6%)
  matrix products  41.8 us (5%)
  starting transfers between devices  27.6 us (4%)
  between operations  13.9 us (2%)
    all_gather x1, waiting for transfers between devices, prefix(): pieces = jax.tree.map(lambda part: lax.all_gather(part, axis), value)  184 us
    all_gather x1, waiting for transfers between devices, experts_layer(): shard_piece = lax.all_gather(arrived, 'ctx', axis=0, tiled=True)  133 us
    reduce_scatter x1, waiting for transfers between devices, experts_layer(): lax.psum_scatter(jnp.einsum('ref,efd->red', hidden, down_weight, preferre...  84.6 us
    all_gather x1, waiting for transfers between devices, softmax_layer(): shard_piece = lax.all_gather(soft_kv, 'ctx', axis=0, tiled=True)  69.8 us
    all_gather x1, blocking collectives, prefix(): pieces = jax.tree.map(lambda part: lax.all_gather(part, axis), value)  68.3 us
    select_n x31, other arithmetic, hop(): jnp.where(position < mine, new, old)  66.2 us
    all_to_all x1, starting transfers between devices, experts_layer(): lax.all_to_all(expert_out, 'exp', split_axis=0, concat_axis=1, tiled=True)  27.5 us
    exp x31, local copies, waits for them, and re-layouts, combine(): jnp.exp(latter[0])[:, None, None] * earlier[1] + latter[1]  21.2 us
  transfers between devices with their start and end apart: 5, of which 5 were waited for; matrix products, arithmetic and copies ran while one was open for 19% of the time, Pallas kernels for 0%

commit v1 on v0

--- a/solution.py
+++ b/solution.py
@@ -124,7 +124,9 @@
     score_scale = 1.0 / math.sqrt(HEAD)
     queries = soft_query.reshape(length, kv_here, group, HEAD)
     query_pos = lax.axis_index("ctx") * length + jnp.arange(length, dtype=jnp.int32)
-    shard_piece = lax.all_gather(soft_kv, "ctx", axis=0, tiled=True)
+    shard_piece = jnp.concatenate(
+        lax.all_to_all(jnp.stack([soft_kv] * lax.axis_size("ctx")), "ctx", 0, 0), axis=0
+    )
     maxima = jnp.full((kv_here, group, length), -jnp.inf, jnp.float32)
     totals = jnp.zeros((kv_here, group, length), jnp.float32)
     running = jnp.zeros((kv_here, group, length, HEAD), jnp.float32)

time: 783 us -> 644 us (0.82)
  waiting for transfers between devices: 476 us -> 306 us
  blocking collectives: 86.9 us -> 112 us
    all_gather x1, waiting for transfers between devices: 184 us -> 88.1 us  [prefix(): pieces = jax.tree.map(lambda part: lax.all_gather(part, axis), value)]
    all_gather x1 -> x0, waiting for transfers between devices: 69.8 us -> none  [softmax_layer(): shard_piece = lax.all_gather(soft_kv, 'ctx', axis=0, tiled=True)]
    all_gather x1, blocking collectives: 68.3 us -> 93.3 us  [prefix(): pieces = jax.tree.map(lambda part: lax.all_gather(part, axis), value)]
  transfers between devices with their start and end apart: 5 -> 5, of which waited for: 5 -> 4; matrix products, arithmetic and copies ran while one was open for 19% -> 23% of each run, Pallas kernels for 0% -> 0%
where the time goes in v1:
time: 644 us; the launch traced here: 641 us
  waiting for transfers between devices  306 us (48%)
  blocking collectives  112 us (17%)
  other arithmetic  88.7 us (14%)
  local copies, waits for them, and re-layouts  45.5 us (7%)
  matrix products  40.1 us (6%)
  starting transfers between devices  34.5 us (5%)
  between operations  14 us (2%)
    all_gather x1, waiting for transfers between devices, experts_layer(): shard_piece = lax.all_gather(arrived, 'ctx', axis=0, tiled=True)  134 us
    all_gather x1, blocking collectives, prefix(): pieces = jax.tree.map(lambda part: lax.all_gather(part, axis), value)  93.3 us
    all_gather x1, waiting for transfers between devices, prefix(): pieces = jax.tree.map(lambda part: lax.all_gather(part, axis), value)  88.1 us
    reduce_scatter x1, waiting for transfers between devices, experts_layer(): lax.psum_scatter(jnp.einsum('ref,efd->red', hidden, down_weight, preferre...  78.8 us
    select_n x31, other arithmetic, hop(): jnp.where(position < mine, new, old)  66.8 us
    all_to_all x1, starting transfers between devices, experts_layer(): lax.all_to_all(expert_out, 'exp', split_axis=0, concat_axis=1, tiled=True)  28.6 us
    exp x31, local copies, waits for them, and re-layouts, combine(): jnp.exp(latter[0])[:, None, None] * earlier[1] + latter[1]  21.4 us
    all_to_all x1, blocking collectives, experts_layer(): lax.all_to_all(outgoing, 'exp', split_axis=1, concat_axis=0, tiled=True)  18.5 us
  transfers between devices with their start and end apart: 5, of which 4 were waited for; matrix products, arithmetic and copies ran while one was open for 23% of the time, Pallas kernels for 0%

profile of v1, /device:TPU:1, one launch (start us, length us, event | category | flops | bytes accessed | tf_op | source)
XLA Modules:
  0.0 641.0 jit_solution(9464602623129970421)
XLA Ops:
  13.0 18.5 %all_to_all.38 = bf16[2,8,6144]{2,0,1:T(2,128)(2,1)} all-to-all(bf16[2,8,6144]{2,0,1:T(2,128)(2,1)S(1)} %copy.122), channel_id=1, replica_groups=mesh['ctx'=32,'exp'=8] {'exp'}, dimensions={1} | all-to-all | bytes 393216 | tf_op jit(solution)/shard_map/all_to_all | solution.py:97
  41.8 2.3 fusion.56
  44.1 134.3 %all-gather.5.cloned.1.call-done = bf16[512,1,6144]{2,0,1:T(8,128)(2,1)} async-done(((bf16[16,1,6144]{2,0,1:T(8,128)(2,1)}), bf16[512,1,6144]{2,0,1:T(8,128)(2,1)}) %all-gather.5.cloned.1.call-update) | async-done | bytes 6291472 | tf_op jit(solution)/shard_map/all_gather | solution.py:98
  178.4 6.0 fusion.16
  187.1 6.3 convolution_bitcast_fusion
  196.2 5.7 all-to-all-start.2
  202.2 93.3 %all-gather.1 = f32[32,1,8]{2,1,0:T(1,128)} all-gather(f32[1,1,8]{2,1,0:T(1,128)S(1)} %copy-done.10), channel_id=1, replica_groups=mesh['ctx'=32,'exp'=8] {'ctx'}, dimensions={0}, use_global_device_ids=true | all-gather | bytes 1056 | tf_op jit(solution)/shard_map/all_gather | solution.py:18
  297.2 7.1 %fusion.3 = (f32[8,128]{1,0:T(8,128)S(1)}, f32[4096,128,8]{1,0,2:T(8,128)}) fusion(pred[128,4096]{0,1:T(8,128)(4,1)S(1)} %iota_compare_fusion, bf16[4096,1,2,128]{3,0,2,1:T(8,128)(2,1)S(1)} %bitcast.197, bf16[128,1024]{1,0:T(8,128)(2,1)S(1)} %copy-done.13), kind=kOutput, calls=%fused_computation.7 | convolution fusion | flops 1086323712 | bytes 18616320 | tf_op jit(solution)/shard_map/tghd,jgd->ghtj/dot_general | solution.py:137
  304.4 9.5 %fusion.1 = f32[8,128]{1,0:T(8,128)S(1)} fusion(f32[4096,128,8]{1,0,2:T(8,128)} %get-tuple-element.152, f32[8,128]{1,0:T(8,128)S(1)} %is-finite_select_fusion, pred[128,4096]{0,1:T(8,128)(4,1)S(1)} %iota_compare_fusion), kind=kLoop, calls=%fused_computation.5 | loop fusion | flops 16776192 | bytes 17309696 | tf_op jit(solution)/shard_map/reduce_sum | solution.py:146
  313.8 8.0 %fusion.53 = bf16[8,128,128]{1,2,0:T(8,128)(2,1)S(1)} fusion(bf16[4096,1,2,128]{3,0,2,1:T(8,128)(2,1)S(1)} %bitcast.198, f32[4096,128,8]{1,0,2:T(8,128)} %get-tuple-element.152, f32[8,128]{1,0:T(8,128)S(1)} %is-finite_select_fusion, pred[128,4096]{0,1:T(8,128)(4,1)S(1)} %iota_compare_fusion, f32[8,128]{1,0:T(8,128)S(1)} %get-tuple-element.146, ...), kind=kOutput, calls=%fused_computation.41 | convolution fusion | flops 1090912256 | bytes 18624512 | tf_op jit(solution)/shard_map/ghtj,jgd->ghtd/dot_general | solution.py:147
  322.7 88.1 %all-gather.7.cloned.1.call-done = f32[256,128,128]{2,1,0:T(8,128)} async-done(((f32[8,128,128]{2,1,0:T(8,128)}), f32[256,128,128]{2,1,0:T(8,128)}) %all-gather.7.cloned.1.call-update) | async-done | bytes 16777232 | tf_op jit(solution)/shard_map/all_gather | solution.py:18
  410.8 88.2 %while.14 = (s32[]{:T(128)}, f32[8,128,128]{2,1,0:T(8,128)}, s32[]{:T(128)}, f32[32,8]{1,0:T(8,128)}, f32[32,8,128,128]{3,2,1,0:T(8,128)}, /*index=5*/s32[]{:T(128)}, s32[]{:T(128)}) while((s32[]{:T(128)}, f32[8,128,128]{2,1,0:T(8,128)}, s32[]{:T(128)}, f32[32,8]{1,0:T(8,128)}, f32[32,8,128,128]{3,2,1,0:T(8,128)}, ...), condition=%wide.region_2.3_spmd.clone, body=%wide.region_1.2_spmd.clone.sunk | while | flops 524292 | bytes 1573065 | solution.py:27
  411.7 2.2 fusion.93
  414.6 2.1 fusion.93
  417.4 2.1 fusion.93
  420.2 2.1 fusion.93
  423.1 2.1 fusion.93
  425.9 2.1 fusion.93
  428.8 2.1 fusion.93
  431.6 2.2 fusion.93
  434.4 2.2 fusion.93
  437.3 2.2 fusion.93
  440.1 2.1 fusion.93
  443.0 2.2 fusion.93
  445.8 2.2 fusion.93
  448.7 2.2 fusion.93
  451.5 2.2 fusion.93
  454.4 2.2 fusion.93
  457.2 2.2 fusion.93
  460.0 2.1 fusion.93
  462.9 2.1 fusion.93
  465.7 2.2 fusion.93
  468.5 2.1 fusion.93
  471.4 2.1 fusion.93
  477.0 2.2 fusion.93
  479.9 2.2 fusion.93
  482.7 2.2 fusion.93
  485.5 2.2 fusion.93
  488.4 2.2 fusion.93
  491.2 2.2 fusion.93
  494.1 2.2 fusion.93
  500.7 2.6 multiply_reduce_fusion
  503.4 78.8 %reduce-scatter.2.cloned.1.call-done = f32[16,1,6144]{2,0,1:T(8,128)} async-done(((f32[512,1,6144]{2,0,1:T(8,128)}), f32[16,1,6144]{2,0,1:T(8,128)}) %reduce-scatter.2.cloned.1.call-update) | async-done | bytes 393232 | tf_op jit(solution)/shard_map/reduce_scatter | solution.py:104
  584.4 2.3 reduce.3
  588.5 28.6 %all-to-all-start.1 = ((bf16[8,2,6144]{2,1,0:T(2,128)(2,1)}), bf16[8,2,6144]{2,1,0:T(2,128)(2,1)}, u32[]{:S(2)}, u32[]{:S(2)}) async-start(bf16[8,2,6144]{2,1,0:T(2,128)(2,1)} %reshape.225), calls=%async_computation.2 | async-start | bytes 393216 | tf_op jit(solution)/shard_map/all_to_all | solution.py:110
  620.9 5.0 all-to-all-done.1
  625.9 2.2 reshape.226
  628.1 2.8 reduce.2
  (109 shorter events, 62.8 us)
Async XLA Ops:
  7.2 179.9 %copy-start = (bf16[1,288,6144]{2,1,0:T(8,128)(2,1)S(1)}, bf16[1,288,6144]{2,1,0:T(8,128)(2,1)}, u32[]{:S(2)}) copy-start(bf16[1,288,6144]{2,1,0:T(8,128)(2,1)} %param.25) | copy-start | bytes 10616836
  7.2 171.2 %all-gather.5.cloned.1.call-start = ((), (), s32[]{:S(2)}) async-start(), calls=%async_computation.4 | async-start | bytes 6488064 | tf_op jit(solution)/shard_map/all_gather | solution.py:98
  33.3 377.6 %all-gather.7.cloned.1.call-start = ((), (), s32[]{:S(2)}) async-start(), calls=%async_computation.6 | async-start | bytes 17301504 | tf_op jit(solution)/shard_map/all_gather | solution.py:18
  44.0 538.2 %reduce-scatter.2.cloned.1.call-start = ((), (), s32[]{:S(2)}) async-start(), calls=%async_computation.5 | async-start | bytes 12976128 | tf_op jit(solution)/shard_map/reduce_scatter | solution.py:104
  178.4 6.0 copy-start.11
  178.4 6.6 %copy-start.12 = (bf16[1,6144,288]{1,2,0:T(8,128)(2,1)S(1)}, bf16[1,6144,288]{1,2,0:T(8,128)(2,1)}, u32[]{:S(2)}) copy-start(bf16[1,6144,288]{1,2,0:T(8,128)(2,1)} %param.24) | copy-start | bytes 10616836
  193.5 0.8 copy-start.8
  193.5 8.5 %copy-start.7 = (f32[128,8]{1,0:T(8,128)S(1)}, f32[128,8]{1,0:T(8,128)}, u32[]{:S(2)}) copy-start(f32[128,8]{1,0:T(8,128)} %get-tuple-element.141) | copy-start | bytes 12292
  193.5 8.5 %copy-start.5 = (f32[128,8]{1,0:T(8,128)S(1)}, f32[128,8]{1,0:T(8,128)}, u32[]{:S(2)}) copy-start(f32[128,8]{1,0:T(8,128)} %reduce_window_sum.11) | copy-start | bytes 12292
  193.5 8.7 %copy-start.10 = (f32[1,1,8]{2,1,0:T(1,128)S(1)}, f32[1,1,8]{2,1,0:T(1,128)}, u32[]{:S(2)}) copy-start(f32[1,1,8]{2,1,0:T(1,128)} %get-tuple-element.144) | copy-start | bytes 100
  193.5 102.1 %copy-start.4 = (bf16[128,1024]{0,1:T(8,128)(2,1)S(1)}, bf16[128,1024]{0,1:T(8,128)(2,1)}, u32[]{:S(2)}) copy-start(bf16[128,1024]{0,1:T(8,128)(2,1)} %copy.137) | copy-start | bytes 786436
  193.5 102.1 %copy-start.6 = (bf16[128,1024]{1,0:T(8,128)(2,1)S(1)}, bf16[128,1024]{1,0:T(8,128)(2,1)}, u32[]{:S(2)}) copy-start(bf16[128,1024]{1,0:T(8,128)(2,1)} %param.15) | copy-start | bytes 786436
  194.3 102.9 %copy-start.13 = (bf16[128,1024]{1,0:T(8,128)(2,1)S(1)}, bf16[128,1024]{1,0:T(8,128)(2,1)}, u32[]{:S(2)}) copy-start(bf16[128,1024]{1,0:T(8,128)(2,1)} %param.26) | copy-start | bytes 786436
  196.2 100.9 %all-to-all-start.2 = ((bf16[32,128,1,2,128]{4,1,3,2,0:T(8,128)(2,1)}), bf16[32,128,1,2,128]{4,1,3,2,0:T(8,128)(2,1)S(1)}, u32[]{:S(2)}, u32[]{:S(2)}) async-start(bf16[32,128,1,2,128]{4,1,3,2,0:T(8,128)(2,1)} %stack.2), calls=%async_computation.3 | async-start | bytes 4194304 | tf_op jit(solution)/shard_map/all_to_all | solution.py:128
  297.2 7.2 %copy-start.2 = (bf16[32,128,1,2,128]{4,1,0,3,2:T(8,128)(2,1)}, bf16[32,128,1,2,128]{4,1,0,3,2:T(8,128)(2,1)S(1)}, u32[]{:S(2)}) copy-start(bf16[32,128,1,2,128]{4,1,0,3,2:T(8,128)(2,1)S(1)} %copy.126) | copy-start | bytes 6291460
  304.3 9.5 %copy-start.3 = (bf16[32,128,1,2,128]{4,1,0,3,2:T(8,128)(2,1)S(1)}, bf16[32,128,1,2,128]{4,1,0,3,2:T(8,128)(2,1)}, u32[]{:S(2)}) copy-start(bf16[32,128,1,2,128]{4,1,0,3,2:T(8,128)(2,1)} %copy-done.2) | copy-start | bytes 6291460
  410.8 223.6 %copy-start.1 = (bf16[1,288,6144]{2,1,0:T(8,128)(2,1)S(1)}, bf16[1,288,6144]{2,1,0:T(8,128)(2,1)}, u32[]{:S(2)}) copy-start(bf16[1,288,6144]{2,1,0:T(8,128)(2,1)} %param.25) | copy-start | bytes 10616836
  410.8 206.3 %copy-start.9 = (f32[1024]{0:T(1024)S(1)}, f32[1024]{0:T(1024)}, u32[]{:S(2)}) copy-start(f32[1024]{0:T(1024)} %param.19) | copy-start | bytes 12292
  588.5 37.4 %all-to-all-start.1 = ((bf16[8,2,6144]{2,1,0:T(2,128)(2,1)}), bf16[8,2,6144]{2,1,0:T(2,128)(2,1)}, u32[]{:S(2)}, u32[]{:S(2)}) async-start(bf16[8,2,6144]{2,1,0:T(2,128)(2,1)} %reshape.225), calls=%async_computation.2 | async-start | bytes 393216 | tf_op jit(solution)/shard_map/all_to_all | solution.py:110
Sparse Core Ops, SparseCore 0:
  33.4 144.9 all-gather.4
  180.2 230.6 all-gather.6
  413.4 168.7 reduce-scatter.1
